TPU v7x, 128 devices: a whole 4x4x4 slice. The times are simulated.
128 devices in a mesh: seq: 16 (over x, z), clu: 8 (over y, core).
Axes of the slice: x: 4, y: 4, z: 4, core: 2. Of those that a mesh axis runs over, the one named last changes fastest.
Arguments:
- queries: bfloat16 [16384, 2048], P(('seq', 'clu')), may hold values from -6 to 6
- key_rows: bfloat16 [16384, 2048], P(('seq', 'clu')), may hold values from -6 to 6
- value_rows: bfloat16 [16384, 2048], P(('seq', 'clu')), may hold values from -6 to 6
- out_grad: bfloat16 [16384, 2048], P(('seq', 'clu')), may hold values from -6 to 6
- cluster_ids: int32 [16384], P(('seq', 'clu')), may hold values from 0 to 127, as said below
Outputs:
- attention_out: bfloat16 [16384, 2048], P(('seq', 'clu'))
- query_grad: bfloat16 [16384, 2048], P(('seq', 'clu'))
- key_grad: bfloat16 [16384, 2048], P(('seq', 'clu'))
- value_grad: bfloat16 [16384, 2048], P(('seq', 'clu'))
Inputs may be any that keep to these rules, and one draw needn't show every extreme that they name: `cluster_ids`: each aligned block of 128 rows (the rows of one device) names any one cluster at most 4 times; in every draw one cluster is named exactly 4 times in every block, so that it holds 512 tokens.
All inputs are finite; a program needn't handle non-finite values.
Results may differ from a plain program's by a relative error of at most 0.02.
Values may be sent and summed in bfloat16 or wider, within the bound.
A program may use at most 128 MiB of HBM per device.

v0:
```python
import math

import jax
import jax.numpy as jnp
from jax import lax
from jax.experimental import pallas as pl
from jax.experimental.pallas import tpu as pltpu
from jax.sharding import PartitionSpec as P

DH = 128
TOK = 128
OVC = 80
SET = 16
FAR = 1e9
MESH = pl.DeviceIdType.MESH


masked = -1e30


def contract_last(left, right):
    return lax.dot_general(
        left, right, (((1,), (1,)), ((), ())), preferred_element_type=jnp.float32
    )


def contract_first(left, right):
    return lax.dot_general(
        left, right, (((0,), (0,)), ((), ())), preferred_element_type=jnp.float32
    )


def softmax_rows(query_head, key_head, allowed, inv_root):
    scores = contract_last(query_head, key_head) * inv_root
    scores = jnp.where(allowed, scores, masked)
    row_max = jnp.max(scores, axis=1, keepdims=True)
    weights = jnp.exp(scores - row_max)
    row_sum = jnp.sum(weights, axis=1, keepdims=True)
    return (weights / row_sum).astype(jnp.bfloat16)


def head_slice(array, head_index):
    return lax.dynamic_slice_in_dim(array, head_index * DH, DH, 1)


def full_capacity(queries, key_rows, value_rows, out_grad, cluster_ids):
    seq_count = lax.axis_size("seq")
    clu_count = lax.axis_size("clu")
    devices = seq_count * clu_count
    tok_rows = queries.shape[0]
    columns = queries.shape[1]
    head_count = columns // DH
    most_rows = 4 * tok_rows // devices
    capacity = most_rows * devices
    inv_root = 1.0 / math.sqrt(DH)
    owners = jnp.arange(devices, dtype=jnp.int32)
    member = (cluster_ids[:, None] == owners[None, :]).astype(jnp.int32)
    running = jnp.cumsum(member, axis=0) - 1
    slot_rank = jnp.sum(member * running, axis=1)
    sent_counts = jnp.sum(member, axis=0).reshape(devices, 1)
    slot_index = cluster_ids * most_rows + slot_rank
    stacked = jnp.concatenate([queries, key_rows, value_rows], axis=1)
    width_in = stacked.shape[1]
    packed = jnp.zeros((devices * most_rows, width_in), jnp.bfloat16).at[slot_index].set(stacked)
    packed = packed.reshape(devices, most_rows, width_in)
    got_rows, got_counts = (
        lax.all_to_all(packed, ("seq", "clu"), split_axis=0, concat_axis=0, tiled=True),
        lax.all_to_all(sent_counts, ("seq", "clu"), split_axis=0, concat_axis=0, tiled=True),
    )
    got_counts = got_counts.reshape(devices)
    starts = jnp.cumsum(got_counts) - got_counts
    live_total = jnp.sum(got_counts)
    within = jnp.arange(most_rows, dtype=jnp.int32)
    target = jnp.where(
        within[None, :] < got_counts[:, None], starts[:, None] + within[None, :], capacity
    )
    target = target.reshape(devices * most_rows)
    gathered = (
        jnp.zeros((capacity, width_in), jnp.bfloat16)
        .at[target]
        .set(got_rows.reshape(devices * most_rows, width_in), mode="drop")
    )
    query_block = gathered[:, :columns]
    key_block = gathered[:, columns : 2 * columns]
    value_block = gathered[:, 2 * columns : 3 * columns]
    positions = jnp.arange(capacity, dtype=jnp.int32)
    allowed = (positions[None, :] <= positions[:, None]) & (positions[None, :] < live_total)

    def forward_head(head_index, mixed_rows):
        weights_low = softmax_rows(
            head_slice(query_block, head_index),
            head_slice(key_block, head_index),
            allowed,
            inv_root,
        )
        out_head = jnp.dot(
            weights_low, head_slice(value_block, head_index), preferred_element_type=jnp.float32
        ).astype(jnp.bfloat16)
        return lax.dynamic_update_slice_in_dim(mixed_rows, out_head, head_index * DH, 1)

    mixed_rows = lax.fori_loop(
        0, head_count, forward_head, jnp.zeros((capacity, columns), jnp.bfloat16)
    )
    back_index = jnp.minimum(target, capacity - 1)
    outgoing = jnp.take(mixed_rows, back_index, axis=0).reshape(devices, most_rows, columns)
    grad_packed = (
        jnp.zeros((devices * most_rows, columns), jnp.bfloat16).at[slot_index].set(out_grad)
    )
    grad_packed = grad_packed.reshape(devices, most_rows, columns)
    returned = lax.all_to_all(outgoing, ("seq", "clu"), split_axis=0, concat_axis=0, tiled=True)
    got_grad = lax.all_to_all(grad_packed, ("seq", "clu"), split_axis=0, concat_axis=0, tiled=True)
    attention_out = jnp.take(returned.reshape(devices * most_rows, columns), slot_index, axis=0)
    grad_block = (
        jnp.zeros((capacity, columns), jnp.bfloat16)
        .at[target]
        .set(got_grad.reshape(devices * most_rows, columns), mode="drop")
    )
    delta_rows = jnp.sum(
        (grad_block.astype(jnp.float32) * mixed_rows.astype(jnp.float32)).reshape(
            capacity, head_count, DH
        ),
        axis=2,
    )

    def backward_head(head_index, grad_rows):
        query_head = head_slice(query_block, head_index)
        key_head = head_slice(key_block, head_index)
        value_head = head_slice(value_block, head_index)
        grad_head = head_slice(grad_block, head_index)
        weights_low = softmax_rows(query_head, key_head, allowed, inv_root)
        prob_grad = contract_last(grad_head, value_head)
        delta_head = lax.dynamic_slice_in_dim(delta_rows, head_index, 1, 1)
        score_grad = (weights_low.astype(jnp.float32) * (prob_grad - delta_head)).astype(
            jnp.bfloat16
        )
        query_part = (
            jnp.dot(score_grad, key_head, preferred_element_type=jnp.float32) * inv_root
        ).astype(jnp.bfloat16)
        key_part = (contract_first(score_grad, query_head) * inv_root).astype(jnp.bfloat16)
        value_part = contract_first(weights_low, grad_head).astype(jnp.bfloat16)
        grad_rows = lax.dynamic_update_slice_in_dim(grad_rows, query_part, head_index * DH, 1)
        grad_rows = lax.dynamic_update_slice_in_dim(
            grad_rows, key_part, columns + head_index * DH, 1
        )
        return lax.dynamic_update_slice_in_dim(
            grad_rows, value_part, 2 * columns + head_index * DH, 1
        )

    grad_rows = lax.fori_loop(
        0, head_count, backward_head, jnp.zeros((capacity, 3 * columns), jnp.bfloat16)
    )
    outgoing_grads = jnp.take(grad_rows, back_index, axis=0).reshape(
        devices, most_rows, 3 * columns
    )
    returned_grads = lax.all_to_all(
        outgoing_grads, ("seq", "clu"), split_axis=0, concat_axis=0, tiled=True
    )
    picked = jnp.take(returned_grads.reshape(devices * most_rows, 3 * columns), slot_index, axis=0)
    return (
        attention_out,
        picked[:, :columns],
        picked[:, columns : 2 * columns],
        picked[:, 2 * columns :],
    )


def bf16_dot(left, right):
    return jnp.dot(left, right, preferred_element_type=jnp.float32)


def flip_perm():
    row = lax.broadcasted_iota(jnp.int32, (SET * 16, SET * 16), 0)
    col = lax.broadcasted_iota(jnp.int32, (SET * 16, SET * 16), 1)
    swapped = (col % 16) * 16 + col // 16
    return (row == swapped).astype(jnp.float32).astype(jnp.bfloat16)


def attend(q, k, v, g, allowed, inv_root):
    raw = jnp.where(allowed, contract_last(k, q), masked)
    most = jnp.max(raw, axis=0, keepdims=True)
    weights = jnp.exp2((raw - most) * (inv_root * math.log2(math.e)))
    prob = weights * (1.0 / jnp.sum(weights, axis=0, keepdims=True))
    prob_low = prob.astype(jnp.bfloat16)
    prob_grad = contract_last(v, g)
    delta = jnp.sum(prob * prob_grad, axis=0, keepdims=True)
    score_grad = (prob * (prob_grad - delta)).astype(jnp.bfloat16)
    out = contract_first(v, prob_low).T.astype(jnp.bfloat16)
    dq = (contract_first(k, score_grad).T * inv_root).astype(jnp.bfloat16)
    dk = bf16_dot(score_grad, q) * inv_root
    dv = bf16_dot(prob_low, g)
    return out, dq, dk, dv


def fast_kernel(
    ids_ref, q_ref, k_ref, v_ref, g_ref,
    out_ref, dq_ref, dk_ref, dv_ref, flag_ref,
    cnt_send, cnt_group, cnt_recv, pack_mat, unpack_mat,
    send_a, send_b, send_c, recv_a, recv_b, recv_c, table,
    over, key_pos, query_pos, pick, onehot, loose, over_res, to_mate, to_block,
    result_a, result_b, result_c, back_a, back_b, back_c,
    ex_send, ex_recv, ex_send2, ex_recv2, ex_ret2, ex_back2, ex_ret1, ex_back1,
    hsend, hrecv, htable, hacc, hresult, hback, inputs, early,
    cnt_send_sem, cnt_sem, cnt2_send_sem, cnt2_sem,
    send_a_sem, recv_a_sem, send_b_sem, recv_b_sem, send_c_sem, recv_c_sem,
    res_a_sem, back_a_sem, res_b_sem, back_b_sem, res_c_sem, back_c_sem,
    ex_send_sem, ex_recv_sem, ex_send2_sem, ex_recv2_sem,
    ex_ret2_sem, ex_back2_sem, ex_ret1_sem, ex_back1_sem,
    hsend_sem, hrecv_sem, hres_sem, hback_sem, input_sem,
):
    seq_at = lax.axis_index("seq")
    clu_at = lax.axis_index("clu")
    groups = lax.axis_size("clu")
    heads = lax.axis_size("seq")
    devices = heads * groups
    me = seq_at * groups + clu_at
    inv_root = 1.0 / math.sqrt(DH)
    is_heavy_owner = lax.rem(seq_at, groups) == clu_at
    at_x, at_z = lax.div(seq_at, 4), lax.rem(seq_at, 4)
    at_y, at_core = lax.div(clu_at, 2), lax.rem(clu_at, 2)

    def by_core(first, second):
        return first + at_core * (second - first)

    eight = []
    for by_x, by_z, by_clu in zip(
        zip((3, 2, 3, 1, 3, 0, 2, 0), (2, 2, 1, 0, 2, 3, 0, 2)),
        zip((0, 0, 2, 3, 1, 2, 3, 1), (2, 2, 0, 1, 3, 0, 0, 2)),
        zip((2, 1, 3, 0, 6, 4, 5, 7), (6, 5, 7, 4, 2, 0, 1, 3)),
    ):
        y = lax.rem(at_y + by_core(by_clu[0] // 2, by_clu[1] // 2), 4)
        core = lax.rem(at_core + by_core(by_clu[0] % 2, by_clu[1] % 2), 2)
        eight.append((by_core(*by_x), by_core(*by_z), y * 2 + core))

    def for_peers(first, count, visit):
        def one_eight(step, carry):
            by = lax.rem(step * 13 + at_core * 12, 16)
            x = at_x + lax.div(by, 4)
            z = at_z + lax.rem(by, 4)
            for j, (more_x, more_z, clu_to) in enumerate(eight):
                seq_to = lax.rem(x + more_x, 4) * 4 + lax.rem(z + more_z, 4)
                if j in (3, 5):
                    pl.when(seq_to * groups + clu_to != me)(lambda: visit(seq_to, clu_to))
                else:
                    visit(seq_to, clu_to)
            return carry

        lax.fori_loop(first, first + count, one_eight, 0)

    def send_steps(first, count, source, target, send_sem, recv_sem):
        def start(seq_to, clu_to):
            pltpu.make_async_remote_copy(
                src_ref=source.at[seq_to * groups + clu_to],
                dst_ref=target,
                send_sem=send_sem,
                recv_sem=recv_sem,
                device_id=(seq_to, clu_to),
                device_id_type=MESH,
            ).start()

        for_peers(first, count, start)

    def send_own(source, target, recv_sem):
        pltpu.make_async_copy(source.at[me], target, recv_sem).start()

    def send_to_all(source, target, send_sem, recv_sem):
        send_steps(0, devices // 8, source, target, send_sem, recv_sem)
        send_own(source, target, recv_sem)

    def wait_bytes(ref, sem):
        pltpu.make_async_copy(ref, ref, sem).wait()

    for array, ref in enumerate((q_ref, k_ref, v_ref, g_ref)):
        pltpu.make_async_copy(ref, inputs.at[array], input_sem).start()
    barrier = pltpu.get_barrier_semaphore()

    def greet(seq_to, clu_to):
        pl.semaphore_signal(barrier, inc=1, device_id=(seq_to, clu_to), device_id_type=MESH)

    for_peers(0, devices // 8, greet)

    sub = lax.broadcasted_iota(jnp.int32, (TOK, TOK), 0)
    lane = lax.broadcasted_iota(jnp.int32, (TOK, TOK), 1)
    sub_f = sub.astype(jnp.float32)
    lane_f = lane.astype(jnp.float32)
    ids_l = jnp.broadcast_to(ids_ref[...].astype(jnp.float32), (TOK, TOK))
    ids_s = ids_l.T
    one = jnp.ones((TOK, TOK), jnp.float32)
    zero = jnp.zeros((TOK, TOK), jnp.float32)
    same = ids_l == ids_s
    rank_l = jnp.sum(jnp.where(same & (sub < lane), one, zero), axis=0, keepdims=True)
    rank_s = jnp.sum(jnp.where(same & (lane < sub), one, zero), axis=1, keepdims=True)
    count_l = jnp.sum(jnp.where(same, one, zero), axis=0, keepdims=True)
    cnt_send[...] = jnp.sum(jnp.where(ids_s == lane_f, one, zero), axis=0, keepdims=True)
    ids_row = ids_l[0:1, :]
    heavy = jnp.min(jnp.where(count_l == 4.0, ids_row, 999.0), axis=1, keepdims=True)
    group_l = jnp.floor(ids_l * (1.0 / 16.0))
    group_s = jnp.floor(ids_s * (1.0 / 16.0))
    earlier = (ids_s < ids_l) | (same & (sub < lane))
    later = (ids_l < ids_s) | (same & (lane < sub))
    before = (group_l == group_s) & (ids_s != heavy) & (rank_s >= 1.0) & earlier
    over_at = jnp.sum(jnp.where(before, one, zero), axis=0, keepdims=True)
    behind = (group_l == group_s) & (ids_l != heavy) & (rank_l >= 1.0) & later
    over_at_s = jnp.sum(jnp.where(behind, one, zero), axis=1, keepdims=True)
    excess_s = (ids_s != heavy) & (rank_s >= 1.0) & (over_at_s >= 4.0)
    excess_at = jnp.sum(jnp.where(excess_s & earlier, one, zero), axis=0, keepdims=True)
    light_l = ids_l != heavy
    slot_group = (sub // 16).astype(jnp.float32)
    in_tile = sub % 16
    over_l = light_l & (rank_l >= 1.0)

    def tile_picks(tile):
        at_slot = (in_tile % 4).astype(jnp.float32)
        if tile < 4:
            cluster = slot_group * 16.0 + at_slot + 4.0 * tile
            taken = (ids_l == cluster) & (rank_l == 0.0) & light_l
        else:
            taken = (group_l == slot_group) & over_l & (over_at == at_slot)
        return [jnp.where(taken & (in_tile // 4 == array), one, zero) for array in range(4)]

    def rest_picks():
        picks = []
        for array in range(4):
            chosen = (ids_l == heavy) & (rank_l == (sub % 4).astype(jnp.float32))
            chosen = chosen & (sub // 4 == array) & (sub < 16)
            beyond = over_l & (over_at >= 4.0) & (excess_at == (sub % 8).astype(jnp.float32))
            beyond = beyond & (sub // 8 == array + 2)
            picks.append(jnp.where(chosen | beyond, one, zero))
        return picks

    def put_pack(at_row, count, picks):
        for array, matrix in enumerate(picks):
            pack_mat[pl.ds(at_row, count), pl.ds(array * TOK, TOK)] = matrix[:count].astype(
                jnp.bfloat16
            )

    put_pack(0, TOK, tile_picks(0))
    put_pack(TOK, TOK, tile_picks(4))
    put_pack(2 * TOK, 48, rest_picks())


    def send_line(source, target, count, at, device, send_sem, recv_sem):
        def one_peer(step, carry):
            to = lax.rem(at + step, count)
            pltpu.make_async_remote_copy(
                src_ref=source(to),
                dst_ref=target,
                send_sem=send_sem,
                recv_sem=recv_sem,
                device_id=device(to),
                device_id_type=MESH,
            ).start()
            return carry

        lax.fori_loop(1, count, one_peer, 0)
        pltpu.make_async_copy(source(at), target, recv_sem).start()

    def along_seq(source, target, send_sem, recv_sem):
        send_line(
            source, target.at[seq_at], heads, seq_at, lambda to: (to, clu_at), send_sem, recv_sem
        )

    def along_clu(source, target, send_sem, recv_sem):
        send_line(
            source, target.at[clu_at], groups, clu_at, lambda to: (seq_at, to), send_sem, recv_sem
        )


    def head_rows(at):
        cols = pl.ds(pl.multiple_of(at * 2 * DH, 2 * DH), 2 * DH)
        return [inputs[array, :, cols] for array in range(4)]

    def put_tile(target, at, tile, packed):
        low = packed.astype(jnp.bfloat16)
        for k in range(2):
            target[pl.ds((2 * at + k) * groups, groups), tile] = low[
                :, k * DH : (k + 1) * DH
            ].reshape(groups, 16, DH)

    def pack_a(at, carry):
        rows = jnp.concatenate(head_rows(at), axis=0)
        packed = bf16_dot(pack_mat[pl.ds(0, 2 * TOK + 48), :], rows)
        put_tile(send_a, at, 0, packed[:TOK])
        put_tile(send_a, at, 1, packed[TOK : 2 * TOK])
        rest = packed[2 * TOK :].astype(jnp.bfloat16)
        for k in range(2):
            hsend[2 * at + k] = rest[:16, k * DH : (k + 1) * DH]
            ex_send[2 * at + k] = rest[16:, k * DH : (k + 1) * DH]
        return carry

    wait_bytes(inputs, input_sem)
    lax.fori_loop(0, heads // 2, pack_a, 0, unroll=2)
    pl.semaphore_wait(barrier, devices - 1)
    along_clu(lambda to: cnt_send, cnt_group, cnt_send_sem, cnt_sem)

    def send_heavy(step, carry):
        head = lax.rem(seq_at + step, heads)
        clu_to = lax.rem(head, groups)

        @pl.when(head * groups + clu_to != me)
        def _():
            pltpu.make_async_remote_copy(
                src_ref=hsend.at[head],
                dst_ref=hrecv.at[me],
                send_sem=hsend_sem,
                recv_sem=hrecv_sem,
                device_id=(head, clu_to),
                device_id_type=MESH,
            ).start()

        @pl.when(head * groups + clu_to == me)
        def _():
            pltpu.make_async_copy(hsend.at[head], hrecv.at[me], hrecv_sem).start()

        return carry

    lax.fori_loop(0, heads, send_heavy, 0)
    along_seq(lambda to: ex_send.at[to], ex_recv, ex_send_sem, ex_recv_sem)
    out_a = (send_a, recv_a.at[me], send_a_sem, recv_a_sem)
    send_steps(0, 4, *out_a)
    wait_bytes(cnt_group, cnt_sem)
    along_seq(lambda to: cnt_group, cnt_recv, cnt2_send_sem, cnt2_sem)
    send_steps(4, devices // 8 - 4, *out_a)
    send_own(send_a, recv_a.at[me], recv_a_sem)

    for tile in range(1, 4):
        put_pack((tile + 1) * TOK + 48, TOK, tile_picks(tile))

    def pack_bc(at, carry):
        rows = jnp.concatenate(head_rows(at), axis=0)
        packed = bf16_dot(pack_mat[pl.ds(2 * TOK + 48, 3 * TOK), :], rows)
        put_tile(send_b, at, 0, packed[:TOK])
        put_tile(send_b, at, 1, packed[TOK : 2 * TOK])
        put_tile(send_c, at, 0, packed[2 * TOK :])
        return carry

    lax.fori_loop(0, heads // 2, pack_bc, 0)

    wait_bytes(cnt_recv, cnt2_sem)
    seen = cnt_recv[...].reshape(TOK, TOK)
    heavies = jnp.min(jnp.where(seen == 4.0, lane_f, 999.0), axis=1, keepdims=True)
    heavy_all = jnp.min(heavies, axis=0, keepdims=True)
    light = lane_f != heavy_all
    more = jnp.where(light, jnp.maximum(seen - 1.0, 0.0), 0.0)
    more_low = more.astype(jnp.bfloat16)
    in_group = jnp.where(sub // 16 == lane, one, zero).astype(jnp.bfloat16)
    ahead = jnp.where(sub < lane, one, zero).astype(jnp.bfloat16)
    prior = jnp.where(lane < sub, one, zero).astype(jnp.bfloat16)
    mates = (lane < sub) & (lane % 8 == sub % 8)
    mates = jnp.where(mates, one, zero).astype(jnp.bfloat16)
    excess = jnp.maximum(bf16_dot(more_low, in_group) - 4.0, 0.0)
    excess_low = excess.astype(jnp.bfloat16)
    excess_off = bf16_dot(excess_low, ahead)
    excess_pre = bf16_dot(mates, excess_low)
    bad = (jnp.sum(excess, axis=1, keepdims=True) > 8.0) | (excess_pre + excess > 16.0)
    bad = bad | (heavies != heavy_all) | (jnp.sum(more, axis=0, keepdims=True) > OVC)
    flag_ref[0, 0] = jnp.max(jnp.where(bad, one, zero)).astype(jnp.int32)

    spot = zero
    for group in range(8):
        off, count, pre = [a[:, group : group + 1] for a in (excess_off, excess, excess_pre)]
        held = (lane_f >= off) & (lane_f < off + count)
        spot = spot + jnp.where(held, lane_f + (group * 16 + 1.0) - off + pre, zero)
    spot = jnp.where(sub % 8 == clu_at, spot, zero).reshape(16, 8, TOK)
    spot = jnp.sum(spot, axis=1).astype(jnp.bfloat16)
    spread8 = jnp.where(lane % 8 == sub, one, zero).astype(jnp.bfloat16)
    spot = jnp.where(lane[:16] // 8 == sub[:16], bf16_dot(spot, spread8), 0.0)
    spot = jnp.sum(spot, axis=0, keepdims=True) - 1.0
    to_mate[...] = jnp.where(sub_f == spot, one, zero).astype(jnp.bfloat16)
    spot = jnp.broadcast_to(spot, (TOK, TOK)).T
    to_block[...] = jnp.where(spot == lane_f, one, zero).astype(jnp.bfloat16)

    wait_bytes(ex_recv, ex_recv_sem)
    held = ex_recv[...].astype(jnp.float32)
    held = [held[:, 8 * a : 8 * a + 8, :].reshape(TOK, DH) for a in range(4)]
    held = jnp.concatenate(held, axis=1).astype(jnp.bfloat16)
    held = bf16_dot(to_mate[...], held).astype(jnp.bfloat16)
    for a in range(4):
        ex_send2[:, a] = held[:, a * DH : (a + 1) * DH].reshape(8, 16, DH)
    along_clu(lambda to: ex_send2.at[to], ex_recv2, ex_send2_sem, ex_recv2_sem)
    send_to_all(send_b, recv_b.at[me], send_b_sem, recv_b_sem)
    send_to_all(send_c, recv_c.at[me], send_c_sem, recv_c_sem)

    valid = jnp.where((seen > 0.0) & light, one, zero).astype(jnp.bfloat16)
    mine = (sub == clu_at * 16 + lane) & (lane < 16)
    mine = jnp.where(mine, one, zero).astype(jnp.bfloat16)
    more_g = bf16_dot(more_low, mine)
    valid_g = bf16_dot(valid, mine)
    more_g_low = more_g.astype(jnp.bfloat16)
    start_g = bf16_dot(prior, more_g_low)
    offset_g = bf16_dot(more_g_low, ahead)
    beyond_g = jnp.maximum(bf16_dot(more_g_low, one.astype(jnp.bfloat16)) - 4.0, 0.0)
    pre_g = bf16_dot(mates, beyond_g.astype(jnp.bfloat16))
    ex_index = lane_f - pre_g + 4.0
    first_row = lax.broadcasted_iota(jnp.int32, (1, TOK), 1).astype(jnp.float32) * 16.0
    in_tile_at = zero
    beyond_at = zero
    for c in range(16):
        count, begin, off, real = [
            a[:, c : c + 1] for a in (more_g, start_g, offset_g, valid_g)
        ]
        place = begin - off + (c * OVC + 1.0)
        held = (lane_f >= off) & (lane_f < off + count) & (lane < 4)
        in_tile_at = in_tile_at + jnp.where(held, lane_f + place, zero)
        held = (ex_index >= off) & (ex_index < off + count) & (ex_index >= 4.0)
        beyond_at = beyond_at + jnp.where(held, ex_index + place, zero)
        held = (lane_f >= begin) & (lane_f < begin + count)
        where = jnp.where(held, sub_f * 16.0 + 1.0 + lane_f - begin, zero)
        where = jnp.sum(where, axis=0, keepdims=True)
        where = jnp.where(where > 0.0, where, FAR)
        query_row = jnp.concatenate([first_row, where], axis=1)
        query_pos[c] = jnp.broadcast_to(query_row, (8, 2 * TOK))
        key_pos[c, pl.ds(0, TOK), :] = jnp.where(real > 0.0, sub_f * 16.0, FAR)
        key_pos[c, pl.ds(TOK, OVC), :] = jnp.broadcast_to(where, (TOK, TOK)).T[:OVC]
    beyond_at = jnp.sum(beyond_at.reshape(16, 8, TOK), axis=0)
    high = jnp.floor(beyond_at * (1.0 / 32.0))
    split = jnp.concatenate([high, beyond_at - high * 32.0], axis=0).astype(jnp.bfloat16)
    spread16 = jnp.where(lane % 16 == sub, one, zero).astype(jnp.bfloat16)
    split = bf16_dot(split, spread16)
    split = jnp.where(lane[:8] // 16 == sub[:8], split[:8] * 32.0 + split[8:], 0.0)
    beyond_row = jnp.sum(split, axis=0, keepdims=True) - 1.0
    tile_rows = in_tile_at.T[0:8, :] - 1.0
    slot_rows = [tile_rows[k : k + 1, :] for k in range(4)] + [beyond_row]
    slot_cols = [in_tile_at[:, k : k + 1] - 1.0 for k in range(4)]
    slot_cols.append(jnp.broadcast_to(beyond_row, (TOK, TOK)).T)

    chunk = 4
    for k in range(5):
        for m in range(16 * OVC // TOK):
            onehot[pl.ds(k * TOK, TOK), pl.ds(m * TOK, TOK)] = jnp.where(
                slot_cols[k] == lane_f + float(m * TOK), one, zero
            ).astype(jnp.bfloat16)
            pick[pl.ds(m * TOK, TOK), pl.ds(k * TOK, TOK)] = jnp.where(
                slot_rows[k] == sub_f + float(m * TOK), one, zero
            ).astype(jnp.bfloat16)

    for at, tile in enumerate((0, 1, 2, None, 3, 4)):
        for array, matrix in enumerate(rest_picks() if tile is None else tile_picks(tile)):
            unpack_mat[pl.ds(array * TOK, TOK), pl.ds(at * TOK, TOK)] = matrix.T.astype(
                jnp.bfloat16
            )

    perm = flip_perm()

    def arrange(source, target, units):
        def two_sets(at, carry):
            blocks = [pl.ds(pl.multiple_of((2 * at + i) * SET, SET), SET) for i in range(2)]
            spots = [(held, unit) for held in blocks for unit in range(units)]
            rows = jnp.concatenate(
                [source(held, unit).reshape(SET * 16, DH) for held, unit in spots], axis=1
            )
            turned = bf16_dot(perm, rows).astype(jnp.bfloat16)
            for i, (held, unit) in enumerate(spots):
                target(held, unit, turned[:, i * DH : (i + 1) * DH].reshape(16, SET, DH))
            return carry

        lax.fori_loop(0, devices // (2 * SET), two_sets, 0, unroll=2)

    def put_table(first):
        def put(blocks, unit, value):
            table[first + unit, :, blocks, :] = value

        return put

    @pl.when(is_heavy_owner)
    def _():
        wait_bytes(hrecv, hrecv_sem)

        def put_heavy(blocks, unit, value):
            htable[:, blocks, :] = value

        arrange(lambda blocks, unit: hrecv[blocks], put_heavy, 1)
        k_h, v_h = [htable[4 * a : 4 * a + 4].reshape(4 * TOK, DH) for a in (1, 2)]
        hacc[...] = jnp.zeros_like(hacc)
        key_sub = lax.broadcasted_iota(jnp.int32, (4 * TOK, TOK), 0)
        key_at = lax.rem(key_sub, TOK) * 4 + lax.div(key_sub, TOK)
        query_at = lax.broadcasted_iota(jnp.int32, (4 * TOK, TOK), 1) * 4

        def heavy_tile(s, carry):
            out, dq, dk, dv = attend(
                htable[s], k_h, v_h, htable[12 + s], key_at <= query_at + s, inv_root
            )
            hacc[2, pl.ds(pl.multiple_of(s * TOK, TOK), TOK)] = out.astype(jnp.float32)
            hacc[3, pl.ds(pl.multiple_of(s * TOK, TOK), TOK)] = dq.astype(jnp.float32)
            hacc[0] += dk
            hacc[1] += dv
            return carry

        lax.fori_loop(0, 4, heavy_tile, 0)
        for array, at in enumerate((2, 3, 0, 1)):
            htable[4 * array : 4 * array + 4] = (
                hacc[at].astype(jnp.bfloat16).reshape(4, TOK, DH)
            )

        def put_hresult(blocks, unit, value):
            hresult[blocks] = value

        arrange(lambda blocks, unit: htable[:, blocks, :], put_hresult, 1)
        send_to_all(hresult, hback.at[seq_at], hres_sem, hback_sem)

    wait_bytes(recv_a, recv_a_sem)
    def put_tile_a(blocks, unit, value):
        table[4 * unit, :, blocks, :] = value

    arrange(lambda blocks, unit: recv_a[blocks, unit], put_tile_a, 2)

    wait_bytes(ex_recv2, ex_recv2_sem)
    for a in range(4):
        cols = pl.ds(a * DH, DH)
        loose[pl.ds(0, 4 * TOK), cols] = table[4, 4 * a : 4 * a + 4].reshape(4 * TOK, DH)
        loose[pl.ds(4 * TOK, TOK), cols] = ex_recv2[:, a].reshape(TOK, DH)

    def gather_chunk(at, carry):
        chosen = pick[pl.ds(pl.multiple_of(at * chunk * OVC, 64), chunk * OVC), :]
        found = bf16_dot(chosen, loose[...]).astype(jnp.bfloat16)
        for c in range(chunk):
            for array in range(4):
                over[array, at * chunk + c] = found[
                    c * OVC : (c + 1) * OVC, array * DH : (array + 1) * DH
                ]
        return carry

    gather_chunk(0, 0)

    pad_rows = jnp.zeros((TOK - OVC, DH), jnp.bfloat16)

    def load_cluster(tile, j):
        c = tile * 4 + j
        rows = [
            jnp.concatenate([table[tile, a * 4 + j], over[a, c]], axis=0) for a in range(4)
        ]
        for a in (0, 3):
            rows[a] = jnp.concatenate([rows[a], pad_rows], axis=0)
        key_at = key_pos[c]
        allowed = jnp.concatenate([key_at, key_at], axis=1) <= query_pos[c, 0:1, :]
        return rows + [allowed]

    def attend_tiles(first, tiles, beside):
        def one_tile(at, carry):
            beside(at)
            tile = first + at
            spots = range(4)
            loaded = [load_cluster(tile, j) for j in spots]
            found = [attend(*arrays, inv_root) for arrays in loaded]
            for j, results in zip(spots, found):
                c = tile * 4 + j
                for a, value in enumerate(results):
                    value = value.astype(jnp.bfloat16)
                    table[tile, a * 4 + j] = value[:TOK]
                    over_res[
                        pl.ds(pl.multiple_of(c * OVC, 16), OVC), pl.ds(a * DH, DH)
                    ] = value[TOK : TOK + OVC]
            return carry

        lax.fori_loop(0, tiles, one_tile, 0)

    def put_in(result):
        def put(blocks, unit, value):
            result[blocks, unit] = value

        return put

    def from_table(first):
        return lambda blocks, unit: table[first + unit, :, blocks, :]

    to_a = (result_a, back_a.at[me], res_a_sem, back_a_sem)
    to_b = (result_b, back_b.at[me], res_b_sem, back_b_sem)
    to_c = (result_c, back_c.at[me], res_c_sem, back_c_sem)
    attend_tiles(0, 1, lambda at: None)
    arrange(from_table(0), put_in(result_a), 1)
    send_own(result_a, back_a.at[me], back_a_sem)
    lax.fori_loop(1, 16 // chunk, gather_chunk, 0)

    wait_bytes(recv_b, recv_b_sem)
    arrange(lambda blocks, unit: recv_b[blocks, unit], put_table(1), 2)
    attend_tiles(1, 2, lambda at: send_steps(at * 8, 8, *to_a))
    arrange(from_table(1), put_in(result_b), 2)
    send_own(result_b, back_b.at[me], back_b_sem)

    wait_bytes(recv_c, recv_c_sem)
    arrange(lambda blocks, unit: recv_c[blocks, 0], put_table(3), 1)
    attend_tiles(3, 1, lambda at: send_steps(0, 16, *to_b))

    found = bf16_dot(onehot[pl.ds(4 * TOK, TOK), :], over_res[...]).astype(jnp.bfloat16)
    for a in range(4):
        ex_ret2[:, a] = found[:, a * DH : (a + 1) * DH].reshape(8, 16, DH)
    along_clu(lambda to: ex_ret2.at[to], ex_back2, ex_ret2_sem, ex_back2_sem)
    found = bf16_dot(onehot[pl.ds(0, 4 * TOK), :], over_res[...]).astype(jnp.bfloat16)
    for a in range(4):
        table[4, 4 * a : 4 * a + 4] = found[:, a * DH : (a + 1) * DH].reshape(4, TOK, DH)
    arrange(from_table(3), put_in(result_c), 2)
    send_steps(0, devices // 16, *to_c)
    send_own(result_c, back_c.at[me], back_c_sem)

    wait_bytes(ex_back2, ex_back2_sem)
    held = [ex_back2[:, a].reshape(TOK, DH) for a in range(4)]
    held = bf16_dot(to_block[...], jnp.concatenate(held, axis=1))
    held = [held[:, a * DH : (a + 1) * DH].reshape(16, 8, DH) for a in range(4)]
    ex_ret1[...] = jnp.concatenate(held, axis=1).astype(jnp.bfloat16)
    along_seq(lambda to: ex_ret1.at[to], ex_back1, ex_ret1_sem, ex_back1_sem)
    send_steps(devices // 16, devices // 16, *to_c)

    def unpack(tiles, rest, first, count):
        sides = []
        for k in range(2):
            sides.append(
                jnp.concatenate(
                    [tile(k).reshape(TOK, DH) for tile in tiles] + [part(k) for part in rest],
                    axis=0,
                )
            )
        return bf16_dot(
            unpack_mat[:, pl.ds(first, count)], jnp.concatenate(sides, axis=1)
        )

    def tile_of(ref, at, tile):
        return lambda k: ref[pl.ds((2 * at + k) * groups, groups), tile]

    def unpack_early(at, carry):
        tiles = [tile_of(back_a, at, 0), tile_of(back_b, at, 0), tile_of(back_b, at, 1)]
        rest = [
            lambda k: hback[2 * at + k],
            lambda k: ex_back1[2 * at + k],
            lambda k: jnp.zeros((TOK - 48, DH), jnp.bfloat16),
        ]
        early[at] = unpack(tiles, rest, 0, 4 * TOK)
        return carry

    def unpack_last(at, carry):
        cols = pl.ds(pl.multiple_of(at * 2 * DH, 2 * DH), 2 * DH)
        tiles = [tile_of(back_c, at, 0), tile_of(back_c, at, 1)]
        found = (early[at] + unpack(tiles, [], 4 * TOK, 2 * TOK)).astype(jnp.bfloat16)
        for array, ref in enumerate((out_ref, dq_ref, dk_ref, dv_ref)):
            ref[:, cols] = found[array * TOK : (array + 1) * TOK]
        return carry

    wait_bytes(hback, hback_sem)
    wait_bytes(back_a, back_a_sem)
    wait_bytes(back_b, back_b_sem)
    wait_bytes(ex_back1, ex_back1_sem)
    lax.fori_loop(0, heads // 2, unpack_early, 0, unroll=2)
    wait_bytes(back_c, back_c_sem)
    lax.fori_loop(0, heads // 2, unpack_last, 0, unroll=2)

    others = pl.ds(0, devices - 1)
    wait_bytes(cnt_group.at[pl.ds(0, groups - 1)], cnt_send_sem)
    wait_bytes(cnt_recv.at[pl.ds(0, heads - 1)], cnt2_send_sem)
    for ref, sem in ((ex_send, ex_send_sem), (ex_ret1, ex_ret1_sem)):
        wait_bytes(ref.at[pl.ds(0, heads - 1)], sem)
    for ref, sem in ((ex_send2, ex_send2_sem), (ex_ret2, ex_ret2_sem)):
        wait_bytes(ref.at[pl.ds(0, groups - 1)], sem)
    wait_bytes(send_a.at[others], send_a_sem)
    wait_bytes(send_b.at[others], send_b_sem)
    wait_bytes(send_c.at[others], send_c_sem)
    wait_bytes(result_a.at[others], res_a_sem)
    wait_bytes(result_b.at[others], res_b_sem)
    wait_bytes(result_c.at[others], res_c_sem)

    @pl.when(is_heavy_owner)
    def _():
        wait_bytes(hsend.at[pl.ds(0, heads - 1)], hsend_sem)
        wait_bytes(hresult.at[others], hres_sem)

    @pl.when(jnp.logical_not(is_heavy_owner))
    def _():
        wait_bytes(hsend, hsend_sem)


def fast_path(queries, key_rows, value_rows, out_grad, cluster_ids):
    tok_rows, columns = queries.shape
    heads = columns // DH
    groups = lax.axis_size("clu")
    devices = lax.axis_size("seq") * groups
    low = jnp.bfloat16
    wide = jnp.float32
    rows = pltpu.VMEM((tok_rows, columns), low)
    vmem = pl.BlockSpec(memory_space=pltpu.VMEM)
    smem = pl.BlockSpec(memory_space=pltpu.SMEM)
    return pl.pallas_call(
        fast_kernel,
        out_shape=[rows] * 4 + [jax.ShapeDtypeStruct((1, 1), jnp.int32)],
        in_specs=[vmem] + [pl.BlockSpec(memory_space=pl.ANY)] * 4,
        out_specs=[vmem] * 4 + [smem],
        scratch_shapes=[
            pltpu.VMEM((1, TOK), wide),
            pltpu.VMEM((groups, 1, TOK), wide),
            pltpu.VMEM((heads, groups, 1, TOK), wide),
            pltpu.VMEM((5 * TOK + 48, 4 * TOK), low),
            pltpu.VMEM((4 * TOK, 6 * TOK), low),
            pltpu.VMEM((devices, 2, 16, DH), low),
            pltpu.VMEM((devices, 2, 16, DH), low),
            pltpu.VMEM((devices, 1, 16, DH), low),
            pltpu.VMEM((devices, 2, 16, DH), low),
            pltpu.VMEM((devices, 2, 16, DH), low),
            pltpu.VMEM((devices, 1, 16, DH), low),
            pltpu.VMEM((5, 16, devices, DH), low),
            pltpu.VMEM((4, 16, OVC, DH), low),
            pltpu.VMEM((16, TOK + OVC, TOK), wide),
            pltpu.VMEM((16, 8, 2 * TOK), wide),
            pltpu.VMEM((16 * OVC, 5 * TOK), low),
            pltpu.VMEM((5 * TOK, 16 * OVC), low),
            pltpu.VMEM((5 * TOK, 4 * DH), low),
            pltpu.VMEM((16 * OVC, 4 * DH), low),
            pltpu.VMEM((TOK, TOK), low),
            pltpu.VMEM((TOK, TOK), low),
            pltpu.VMEM((devices, 1, 16, DH), low),
            pltpu.VMEM((devices, 2, 16, DH), low),
            pltpu.VMEM((devices, 2, 16, DH), low),
            pltpu.VMEM((devices, 1, 16, DH), low),
            pltpu.VMEM((devices, 2, 16, DH), low),
            pltpu.VMEM((devices, 2, 16, DH), low),
            pltpu.VMEM((heads, 32, DH), low),
            pltpu.VMEM((heads, 32, DH), low),
            pltpu.VMEM((groups, 4, 16, DH), low),
            pltpu.VMEM((groups, 4, 16, DH), low),
            pltpu.VMEM((groups, 4, 16, DH), low),
            pltpu.VMEM((groups, 4, 16, DH), low),
            pltpu.VMEM((heads, 32, DH), low),
            pltpu.VMEM((heads, 32, DH), low),
            pltpu.VMEM((heads, 16, DH), low),
            pltpu.VMEM((devices, 16, DH), low),
            pltpu.VMEM((16, devices, DH), low),
            pltpu.VMEM((4, 4 * TOK, DH), wide),
            pltpu.VMEM((devices, 16, DH), low),
            pltpu.VMEM((heads, 16, DH), low),
            pltpu.VMEM((4, tok_rows, columns), low),
            pltpu.VMEM((heads // 2, 4 * tok_rows, 2 * DH), wide),
        ]
        + [pltpu.SemaphoreType.DMA] * 29,
        compiler_params=pltpu.CompilerParams(
            collective_id=0, has_side_effects=True, vmem_limit_bytes=44 * 1024 * 1024
        ),
    )(cluster_ids.reshape(1, tok_rows), queries, key_rows, value_rows, out_grad)


def copy_kernel(*refs):
    sem = refs[-1]
    copies = [
        pltpu.make_async_copy(refs[i], refs[4 + i], sem.at[i]) for i in range(4)
    ]
    for copy in copies:
        copy.start()
    for copy in copies:
        copy.wait()


def copy_out(arrays):
    anywhere = pl.BlockSpec(memory_space=pl.ANY)
    return pl.pallas_call(
        copy_kernel,
        out_shape=[pltpu.HBM(a.shape, a.dtype) for a in arrays],
        in_specs=[anywhere] * 4,
        out_specs=[anywhere] * 4,
        scratch_shapes=[pltpu.SemaphoreType.DMA((4,))],
    )(*arrays)


def per_device(queries, key_rows, value_rows, out_grad, cluster_ids):
    arrays = (queries, key_rows, value_rows, out_grad, cluster_ids)
    *fast, flag = fast_path(*arrays)
    return lax.cond(
        flag.reshape(()) != 0,
        lambda arrays, fast: full_capacity(*arrays),
        lambda arrays, fast: tuple(copy_out(fast)),
        arrays,
        tuple(fast),
    )


def solution(mesh):
    in_specs = (
        P(("seq", "clu"), None),
        P(("seq", "clu"), None),
        P(("seq", "clu"), None),
        P(("seq", "clu"), None),
        P(("seq", "clu")),
    )
    out_specs = (
        P(("seq", "clu"), None),
        P(("seq", "clu"), None),
        P(("seq", "clu"), None),
        P(("seq", "clu"), None),
    )
    return jax.shard_map(
        per_device, mesh=mesh, in_specs=in_specs, out_specs=out_specs, check_vma=False
    )
```

profile of v0, /device:TPU:1, one launch (start us, length us, event | category | flops | bytes accessed | tf_op | source)
XLA Modules:
  0.0 94.1 jit_solution(10847570839070814886)
XLA Ops:
  0.6 0.0 copy-start.2
  0.6 0.0 copy-start.1
  0.7 0.0 copy-start
  0.7 91.0 %shard_map.92 = (bf16[128,2048]{1,0:T(8,128)(2,1)S(1)}, bf16[128,2048]{1,0:T(8,128)(2,1)S(1)}, bf16[128,2048]{1,0:T(8,128)(2,1)S(1)}, bf16[128,2048]{1,0:T(8,128)(2,1)S(1)}, s32[1,1]{1,0:T(1,128)}) custom-call(s32[1,128]{1,0:T(1,128)} %bitcast.25, bf16[128,2048]{1,0:T(8,128)(2,1)} %q_ref.1, bf16[128,2048]{1,0:T(8,128)(2,1)} %k_ref.1, ...), custom_call_target="tpu_custom_call" | custom-call | tf_op jit(solution)/shard_map/pallas_call | solution.py:778
  92.3 0.0 copy-done.2
  92.3 0.0 copy-done.1
  92.4 0.0 copy-done
  92.4 1.5 %conditional.1 = ((bf16[128,2048]{1,0:T(8,128)(2,1)}, bf16[128,2048]{1,0:T(8,128)(2,1)}, bf16[128,2048]{1,0:T(8,128)(2,1)}, bf16[128,2048]{1,0:T(8,128)(2,1)})) conditional(s32[]{:T(128)} %bitcast.5, (bf16[128,2048]{1,0:T(8,128)(2,1)S(1)}, bf16[128,2048]{1,0:T(8,128)(2,1)S(1)}, bf16[128,2048]{1,0:T(8,128)(2,1)S(1)}, ...), branch_computations={%region_0.0_spmd, %region_1.20_spmd} | conditional | flops 493620608 | bytes 234142496 | solution.py:860
  92.4 1.3 %branch_0_fun.1 = (bf16[128,2048]{1,0:T(8,128)(2,1)}, bf16[128,2048]{1,0:T(8,128)(2,1)}, bf16[128,2048]{1,0:T(8,128)(2,1)}, bf16[128,2048]{1,0:T(8,128)(2,1)}) custom-call(bf16[128,2048]{1,0:T(8,128)(2,1)S(1)} %get-tuple-element.308.refs_0_, bf16[128,2048]{1,0:T(8,128)(2,1)S(1)} %get-tuple-element.309.refs_1_, ...), custom_call_target="tpu_custom_call" | custom-call | tf_op jit(solution)/shard_map/cond/branch_0_fun/pallas_call | solution.py:848
Async XLA Ops:
  0.6 91.7 %copy-start.2 = (s32[128]{0:T(128)S(1)}, s32[128]{0:T(128)}, u32[]{:S(2)}) copy-start(s32[128]{0:T(128)} %param.15) | copy-start | bytes 1540
  0.6 91.7 %copy-start.1 = (bf16[128,2048]{1,0:T(8,128)(2,1)S(1)}, bf16[128,2048]{1,0:T(8,128)(2,1)}, u32[]{:S(2)}) copy-start(bf16[128,2048]{1,0:T(8,128)(2,1)} %k_ref.1) | copy-start | bytes 1572868
  0.7 91.7 %copy-start = (bf16[128,2048]{1,0:T(8,128)(2,1)S(1)}, bf16[128,2048]{1,0:T(8,128)(2,1)}, u32[]{:S(2)}) copy-start(bf16[128,2048]{1,0:T(8,128)(2,1)} %q_ref.1) | copy-start | bytes 1572868
where the time goes:
time: 94.2 us; the launch traced here: 94.1 us
  Pallas kernels  92.3 us (98%)
  between operations  1.56 us (2%)
    pallas_call x1, Pallas kernels, fast_path(): pl.pallas_call(fast_kernel, out_shape=[rows] * 4 + [jax.ShapeDtypeStruct(...  91 us

commit v1 on v0

--- a/solution.py
+++ b/solution.py
@@ -388,7 +388,7 @@
         return carry
 
     wait_bytes(inputs, input_sem)
-    lax.fori_loop(0, heads // 2, pack_a, 0, unroll=2)
+    lax.fori_loop(0, heads // 2, pack_a, 0, unroll=4)
     pl.semaphore_wait(barrier, devices - 1)
     along_clu(lambda to: cnt_send, cnt_group, cnt_send_sem, cnt_sem)
 
@@ -634,9 +634,8 @@
         allowed = jnp.concatenate([key_at, key_at], axis=1) <= query_pos[c, 0:1, :]
         return rows + [allowed]
 
-    def attend_tiles(first, tiles, beside):
+    def attend_tiles(first, tiles):
         def one_tile(at, carry):
-            beside(at)
             tile = first + at
             spots = range(4)
             loaded = [load_cluster(tile, j) for j in spots]
@@ -665,20 +664,20 @@
     to_a = (result_a, back_a.at[me], res_a_sem, back_a_sem)
     to_b = (result_b, back_b.at[me], res_b_sem, back_b_sem)
     to_c = (result_c, back_c.at[me], res_c_sem, back_c_sem)
-    attend_tiles(0, 1, lambda at: None)
+    attend_tiles(0, 1)
     arrange(from_table(0), put_in(result_a), 1)
-    send_own(result_a, back_a.at[me], back_a_sem)
+    send_to_all(*to_a)
     lax.fori_loop(1, 16 // chunk, gather_chunk, 0)
 
     wait_bytes(recv_b, recv_b_sem)
     arrange(lambda blocks, unit: recv_b[blocks, unit], put_table(1), 2)
-    attend_tiles(1, 2, lambda at: send_steps(at * 8, 8, *to_a))
+    attend_tiles(1, 2)
     arrange(from_table(1), put_in(result_b), 2)
-    send_own(result_b, back_b.at[me], back_b_sem)
+    send_to_all(*to_b)
 
     wait_bytes(recv_c, recv_c_sem)
     arrange(lambda blocks, unit: recv_c[blocks, 0], put_table(3), 1)
-    attend_tiles(3, 1, lambda at: send_steps(0, 16, *to_b))
+    attend_tiles(3, 1)
 
     found = bf16_dot(onehot[pl.ds(4 * TOK, TOK), :], over_res[...]).astype(jnp.bfloat16)
     for a in range(4):

time: 94.2 us -> 92.7 us (0.984); the launches traced: 94.1 us -> 91 us
  Pallas kernels: 92.3 us -> 89.2 us
    pallas_call x1, Pallas kernels: 91 us -> 87.8 us  [fast_path(): pl.pallas_call(fast_kernel, out_shape=[rows] * 4 + [jax.ShapeDtypeStruct(...]
where the time goes in v1:
time: 92.7 us; the launch traced here: 91 us
  Pallas kernels  89.2 us (96%)
  between operations  1.58 us (2%)
    pallas_call x1, Pallas kernels, fast_path(): pl.pallas_call(fast_kernel, out_shape=[rows] * 4 + [jax.ShapeDtypeStruct(...  87.8 us

profile of v1, /device:TPU:1, one launch (start us, length us, event | category | flops | bytes accessed | tf_op | source)
XLA Modules:
  0.0 91.0 jit_solution(3854777298927729325)
XLA Ops:
  0.6 0.0 copy-start.2
  0.6 0.0 copy-start.1
  0.7 0.0 copy-start
  0.7 87.8 %shard_map.92 = (bf16[128,2048]{1,0:T(8,128)(2,1)S(1)}, bf16[128,2048]{1,0:T(8,128)(2,1)S(1)}, bf16[128,2048]{1,0:T(8,128)(2,1)S(1)}, bf16[128,2048]{1,0:T(8,128)(2,1)S(1)}, s32[1,1]{1,0:T(1,128)}) custom-call(s32[1,128]{1,0:T(1,128)} %bitcast.25, bf16[128,2048]{1,0:T(8,128)(2,1)} %q_ref.1, bf16[128,2048]{1,0:T(8,128)(2,1)} %k_ref.1, ...), custom_call_target="tpu_custom_call" | custom-call | tf_op jit(solution)/shard_map/pallas_call | solution.py:777
  89.2 0.0 copy-done.2
  89.2 0.0 copy-done.1
  89.2 0.0 copy-done
  89.2 1.6 %conditional.1 = ((bf16[128,2048]{1,0:T(8,128)(2,1)}, bf16[128,2048]{1,0:T(8,128)(2,1)}, bf16[128,2048]{1,0:T(8,128)(2,1)}, bf16[128,2048]{1,0:T(8,128)(2,1)})) conditional(s32[]{:T(128)} %bitcast.5, (bf16[128,2048]{1,0:T(8,128)(2,1)S(1)}, bf16[128,2048]{1,0:T(8,128)(2,1)S(1)}, bf16[128,2048]{1,0:T(8,128)(2,1)S(1)}, ...), branch_computations={%region_0.0_spmd, %region_1.20_spmd} | conditional | flops 493620608 | bytes 234142496 | solution.py:859
  89.2 1.3 %branch_0_fun.1 = (bf16[128,2048]{1,0:T(8,128)(2,1)}, bf16[128,2048]{1,0:T(8,128)(2,1)}, bf16[128,2048]{1,0:T(8,128)(2,1)}, bf16[128,2048]{1,0:T(8,128)(2,1)}) custom-call(bf16[128,2048]{1,0:T(8,128)(2,1)S(1)} %get-tuple-element.308.refs_0_, bf16[128,2048]{1,0:T(8,128)(2,1)S(1)} %get-tuple-element.309.refs_1_, ...), custom_call_target="tpu_custom_call" | custom-call | tf_op jit(solution)/shard_map/cond/branch_0_fun/pallas_call | solution.py:847
Async XLA Ops:
  0.6 88.6 %copy-start.2 = (s32[128]{0:T(128)S(1)}, s32[128]{0:T(128)}, u32[]{:S(2)}) copy-start(s32[128]{0:T(128)} %param.15) | copy-start | bytes 1540
  0.6 88.6 %copy-start.1 = (bf16[128,2048]{1,0:T(8,128)(2,1)S(1)}, bf16[128,2048]{1,0:T(8,128)(2,1)}, u32[]{:S(2)}) copy-start(bf16[128,2048]{1,0:T(8,128)(2,1)} %k_ref.1) | copy-start | bytes 1572868
  0.7 88.6 %copy-start = (bf16[128,2048]{1,0:T(8,128)(2,1)S(1)}, bf16[128,2048]{1,0:T(8,128)(2,1)}, u32[]{:S(2)}) copy-start(bf16[128,2048]{1,0:T(8,128)(2,1)} %q_ref.1) | copy-start | bytes 1572868

commit v2 on v1

--- a/solution.py
+++ b/solution.py
@@ -338,9 +338,16 @@
     put_pack(2 * TOK, 48, rest_picks())
 
 
-    def send_line(source, target, count, at, device, send_sem, recv_sem):
+    def seq_step(step):
+        offset = lax.rem(step * 7, 16)
+        return by_core(offset, lax.rem(offset, 4) * 4 + lax.div(offset, 4))
+
+    def clu_step(step):
+        return lax.rem(step * (3 + 2 * at_core), 8)
+
+    def send_line(source, target, count, at, order, device, send_sem, recv_sem):
         def one_peer(step, carry):
-            to = lax.rem(at + step, count)
+            to = lax.rem(at + order(step), count)
             pltpu.make_async_remote_copy(
                 src_ref=source(to),
                 dst_ref=target,
@@ -356,12 +363,14 @@
 
     def along_seq(source, target, send_sem, recv_sem):
         send_line(
-            source, target.at[seq_at], heads, seq_at, lambda to: (to, clu_at), send_sem, recv_sem
+            source, target.at[seq_at], heads, seq_at, seq_step,
+            lambda to: (to, clu_at), send_sem, recv_sem,
         )
 
     def along_clu(source, target, send_sem, recv_sem):
         send_line(
-            source, target.at[clu_at], groups, clu_at, lambda to: (seq_at, to), send_sem, recv_sem
+            source, target.at[clu_at], groups, clu_at, clu_step,
+            lambda to: (seq_at, to), send_sem, recv_sem,
         )
 
 
@@ -393,7 +402,7 @@
     along_clu(lambda to: cnt_send, cnt_group, cnt_send_sem, cnt_sem)
 
     def send_heavy(step, carry):
-        head = lax.rem(seq_at + step, heads)
+        head = lax.rem(seq_at + seq_step(step), heads)
         clu_to = lax.rem(head, groups)
 
         @pl.when(head * groups + clu_to != me)

time: 92.7 us -> 93 us (level)
  the two profiles are of different devices: /device:TPU:1 before, /device:TPU:3 now
where the time goes in v2:
time: 93 us; the launch traced here: 92.9 us
  Pallas kernels  91.2 us (98%)
  between operations  1.56 us (2%)
    pallas_call x1, Pallas kernels, fast_path(): pl.pallas_call(fast_kernel, out_shape=[rows] * 4 + [jax.ShapeDtypeStruct(...  89.8 us

profile of v2, /device:TPU:3, one launch (start us, length us, event | category | flops | bytes accessed | tf_op | source)
XLA Modules:
  0.0 92.9 jit_solution(9978107645778242402)
XLA Ops:
  0.6 0.0 copy-start.2
  0.6 0.0 copy-start.1
  0.7 0.0 copy-start
  0.7 89.8 %shard_map.92 = (bf16[128,2048]{1,0:T(8,128)(2,1)S(1)}, bf16[128,2048]{1,0:T(8,128)(2,1)S(1)}, bf16[128,2048]{1,0:T(8,128)(2,1)S(1)}, bf16[128,2048]{1,0:T(8,128)(2,1)S(1)}, s32[1,1]{1,0:T(1,128)}) custom-call(s32[1,128]{1,0:T(1,128)} %bitcast.25, bf16[128,2048]{1,0:T(8,128)(2,1)} %q_ref.1, bf16[128,2048]{1,0:T(8,128)(2,1)} %k_ref.1, ...), custom_call_target="tpu_custom_call" | custom-call | tf_op jit(solution)/shard_map/pallas_call | solution.py:786
  91.2 0.0 copy-done.2
  91.2 0.0 copy-done.1
  91.2 0.0 copy-done
  91.2 1.5 %conditional.1 = ((bf16[128,2048]{1,0:T(8,128)(2,1)}, bf16[128,2048]{1,0:T(8,128)(2,1)}, bf16[128,2048]{1,0:T(8,128)(2,1)}, bf16[128,2048]{1,0:T(8,128)(2,1)})) conditional(s32[]{:T(128)} %bitcast.5, (bf16[128,2048]{1,0:T(8,128)(2,1)S(1)}, bf16[128,2048]{1,0:T(8,128)(2,1)S(1)}, bf16[128,2048]{1,0:T(8,128)(2,1)S(1)}, ...), branch_computations={%region_0.0_spmd, %region_1.20_spmd} | conditional | flops 493620608 | bytes 234142496 | solution.py:868
  91.2 1.3 %branch_0_fun.1 = (bf16[128,2048]{1,0:T(8,128)(2,1)}, bf16[128,2048]{1,0:T(8,128)(2,1)}, bf16[128,2048]{1,0:T(8,128)(2,1)}, bf16[128,2048]{1,0:T(8,128)(2,1)}) custom-call(bf16[128,2048]{1,0:T(8,128)(2,1)S(1)} %get-tuple-element.308.refs_0_, bf16[128,2048]{1,0:T(8,128)(2,1)S(1)} %get-tuple-element.309.refs_1_, ...), custom_call_target="tpu_custom_call" | custom-call | tf_op jit(solution)/shard_map/cond/branch_0_fun/pallas_call | solution.py:856
Async XLA Ops:
  0.6 90.5 %copy-start.2 = (s32[128]{0:T(128)S(1)}, s32[128]{0:T(128)}, u32[]{:S(2)}) copy-start(s32[128]{0:T(128)} %param.15) | copy-start | bytes 1540
  0.6 90.5 %copy-start.1 = (bf16[128,2048]{1,0:T(8,128)(2,1)S(1)}, bf16[128,2048]{1,0:T(8,128)(2,1)}, u32[]{:S(2)}) copy-start(bf16[128,2048]{1,0:T(8,128)(2,1)} %k_ref.1) | copy-start | bytes 1572868
  0.7 90.5 %copy-start = (bf16[128,2048]{1,0:T(8,128)(2,1)S(1)}, bf16[128,2048]{1,0:T(8,128)(2,1)}, u32[]{:S(2)}) copy-start(bf16[128,2048]{1,0:T(8,128)(2,1)} %q_ref.1) | copy-start | bytes 1572868

commit v3 on v1

--- a/solution.py
+++ b/solution.py
@@ -533,7 +533,7 @@
                 slot_rows[k] == sub_f + float(m * TOK), one, zero
             ).astype(jnp.bfloat16)
 
-    for at, tile in enumerate((0, 1, 2, None, 3, 4)):
+    for at, tile in enumerate((0, 1, 2, 3, 4, None)):
         for array, matrix in enumerate(rest_picks() if tile is None else tile_picks(tile)):
             unpack_mat[pl.ds(array * TOK, TOK), pl.ds(at * TOK, TOK)] = matrix.T.astype(
                 jnp.bfloat16
@@ -560,42 +560,6 @@
             table[first + unit, :, blocks, :] = value
 
         return put
-
-    @pl.when(is_heavy_owner)
-    def _():
-        wait_bytes(hrecv, hrecv_sem)
-
-        def put_heavy(blocks, unit, value):
-            htable[:, blocks, :] = value
-
-        arrange(lambda blocks, unit: hrecv[blocks], put_heavy, 1)
-        k_h, v_h = [htable[4 * a : 4 * a + 4].reshape(4 * TOK, DH) for a in (1, 2)]
-        hacc[...] = jnp.zeros_like(hacc)
-        key_sub = lax.broadcasted_iota(jnp.int32, (4 * TOK, TOK), 0)
-        key_at = lax.rem(key_sub, TOK) * 4 + lax.div(key_sub, TOK)
-        query_at = lax.broadcasted_iota(jnp.int32, (4 * TOK, TOK), 1) * 4
-
-        def heavy_tile(s, carry):
-            out, dq, dk, dv = attend(
-                htable[s], k_h, v_h, htable[12 + s], key_at <= query_at + s, inv_root
-            )
-            hacc[2, pl.ds(pl.multiple_of(s * TOK, TOK), TOK)] = out.astype(jnp.float32)
-            hacc[3, pl.ds(pl.multiple_of(s * TOK, TOK), TOK)] = dq.astype(jnp.float32)
-            hacc[0] += dk
-            hacc[1] += dv
-            return carry
-
-        lax.fori_loop(0, 4, heavy_tile, 0)
-        for array, at in enumerate((2, 3, 0, 1)):
-            htable[4 * array : 4 * array + 4] = (
-                hacc[at].astype(jnp.bfloat16).reshape(4, TOK, DH)
-            )
-
-        def put_hresult(blocks, unit, value):
-            hresult[blocks] = value
-
-        arrange(lambda blocks, unit: htable[:, blocks, :], put_hresult, 1)
-        send_to_all(hresult, hback.at[seq_at], hres_sem, hback_sem)
 
     wait_bytes(recv_a, recv_a_sem)
     def put_tile_a(blocks, unit, value):
@@ -698,6 +662,42 @@
     along_seq(lambda to: ex_ret1.at[to], ex_back1, ex_ret1_sem, ex_back1_sem)
     send_steps(devices // 16, devices // 16, *to_c)
 
+    @pl.when(is_heavy_owner)
+    def _():
+        wait_bytes(hrecv, hrecv_sem)
+
+        def put_heavy(blocks, unit, value):
+            htable[:, blocks, :] = value
+
+        arrange(lambda blocks, unit: hrecv[blocks], put_heavy, 1)
+        k_h, v_h = [htable[4 * a : 4 * a + 4].reshape(4 * TOK, DH) for a in (1, 2)]
+        hacc[...] = jnp.zeros_like(hacc)
+        key_sub = lax.broadcasted_iota(jnp.int32, (4 * TOK, TOK), 0)
+        key_at = lax.rem(key_sub, TOK) * 4 + lax.div(key_sub, TOK)
+        query_at = lax.broadcasted_iota(jnp.int32, (4 * TOK, TOK), 1) * 4
+
+        def heavy_tile(s, carry):
+            out, dq, dk, dv = attend(
+                htable[s], k_h, v_h, htable[12 + s], key_at <= query_at + s, inv_root
+            )
+            hacc[2, pl.ds(pl.multiple_of(s * TOK, TOK), TOK)] = out.astype(jnp.float32)
+            hacc[3, pl.ds(pl.multiple_of(s * TOK, TOK), TOK)] = dq.astype(jnp.float32)
+            hacc[0] += dk
+            hacc[1] += dv
+            return carry
+
+        lax.fori_loop(0, 4, heavy_tile, 0)
+        for array, at in enumerate((2, 3, 0, 1)):
+            htable[4 * array : 4 * array + 4] = (
+                hacc[at].astype(jnp.bfloat16).reshape(4, TOK, DH)
+            )
+
+        def put_hresult(blocks, unit, value):
+            hresult[blocks] = value
+
+        arrange(lambda blocks, unit: htable[:, blocks, :], put_hresult, 1)
+        send_to_all(hresult, hback.at[seq_at], hres_sem, hback_sem)
+
     def unpack(tiles, rest, first, count):
         sides = []
         for k in range(2):
@@ -716,27 +716,27 @@
 
     def unpack_early(at, carry):
         tiles = [tile_of(back_a, at, 0), tile_of(back_b, at, 0), tile_of(back_b, at, 1)]
+        early[at] = unpack(tiles, [], 0, 3 * TOK)
+        return carry
+
+    def unpack_last(at, carry):
+        cols = pl.ds(pl.multiple_of(at * 2 * DH, 2 * DH), 2 * DH)
+        tiles = [tile_of(back_c, at, 0), tile_of(back_c, at, 1)]
         rest = [
             lambda k: hback[2 * at + k],
             lambda k: ex_back1[2 * at + k],
             lambda k: jnp.zeros((TOK - 48, DH), jnp.bfloat16),
         ]
-        early[at] = unpack(tiles, rest, 0, 4 * TOK)
-        return carry
-
-    def unpack_last(at, carry):
-        cols = pl.ds(pl.multiple_of(at * 2 * DH, 2 * DH), 2 * DH)
-        tiles = [tile_of(back_c, at, 0), tile_of(back_c, at, 1)]
-        found = (early[at] + unpack(tiles, [], 4 * TOK, 2 * TOK)).astype(jnp.bfloat16)
+        found = (early[at] + unpack(tiles, rest, 3 * TOK, 3 * TOK)).astype(jnp.bfloat16)
         for array, ref in enumerate((out_ref, dq_ref, dk_ref, dv_ref)):
             ref[:, cols] = found[array * TOK : (array + 1) * TOK]
         return carry
 
-    wait_bytes(hback, hback_sem)
     wait_bytes(back_a, back_a_sem)
     wait_bytes(back_b, back_b_sem)
+    lax.fori_loop(0, heads // 2, unpack_early, 0, unroll=2)
     wait_bytes(ex_back1, ex_back1_sem)
-    lax.fori_loop(0, heads // 2, unpack_early, 0, unroll=2)
+    wait_bytes(hback, hback_sem)
     wait_bytes(back_c, back_c_sem)
     lax.fori_loop(0, heads // 2, unpack_last, 0, unroll=2)
 

time: 92.7 us -> 93.5 us (level); the launches traced: 91 us -> 93 us
  Pallas kernels: 89.2 us -> 91.2 us
    pallas_call x1, Pallas kernels: 87.8 us -> 89.8 us  [fast_path(): pl.pallas_call(fast_kernel, out_shape=[rows] * 4 + [jax.ShapeDtypeStruct(...]
where the time goes in v3:
time: 93.5 us; the launch traced here: 93 us
  Pallas kernels  91.2 us (98%)
  between operations  1.58 us (2%)
    pallas_call x1, Pallas kernels, fast_path(): pl.pallas_call(fast_kernel, out_shape=[rows] * 4 + [jax.ShapeDtypeStruct(...  89.8 us

profile of v3, /device:TPU:1, one launch (start us, length us, event | category | flops | bytes accessed | tf_op | source)
XLA Modules:
  0.0 93.0 jit_solution(2113103130905309211)
XLA Ops:
  0.6 0.0 copy-start.2
  0.6 0.0 copy-start.1
  0.7 0.0 copy-start
  0.7 89.8 %shard_map.92 = (bf16[128,2048]{1,0:T(8,128)(2,1)S(1)}, bf16[128,2048]{1,0:T(8,128)(2,1)S(1)}, bf16[128,2048]{1,0:T(8,128)(2,1)S(1)}, bf16[128,2048]{1,0:T(8,128)(2,1)S(1)}, s32[1,1]{1,0:T(1,128)}) custom-call(s32[1,128]{1,0:T(1,128)} %bitcast.25, bf16[128,2048]{1,0:T(8,128)(2,1)} %q_ref.1, bf16[128,2048]{1,0:T(8,128)(2,1)} %k_ref.1, ...), custom_call_target="tpu_custom_call" | custom-call | tf_op jit(solution)/shard_map/pallas_call | solution.py:777
  91.2 0.0 copy-done.2
  91.2 0.0 copy-done.1
  91.2 0.0 copy-done
  91.2 1.6 %conditional.1 = ((bf16[128,2048]{1,0:T(8,128)(2,1)}, bf16[128,2048]{1,0:T(8,128)(2,1)}, bf16[128,2048]{1,0:T(8,128)(2,1)}, bf16[128,2048]{1,0:T(8,128)(2,1)})) conditional(s32[]{:T(128)} %bitcast.5, (bf16[128,2048]{1,0:T(8,128)(2,1)S(1)}, bf16[128,2048]{1,0:T(8,128)(2,1)S(1)}, bf16[128,2048]{1,0:T(8,128)(2,1)S(1)}, ...), branch_computations={%region_0.0_spmd, %region_1.20_spmd} | conditional | flops 493620608 | bytes 234142496 | solution.py:859
  91.2 1.3 %branch_0_fun.1 = (bf16[128,2048]{1,0:T(8,128)(2,1)}, bf16[128,2048]{1,0:T(8,128)(2,1)}, bf16[128,2048]{1,0:T(8,128)(2,1)}, bf16[128,2048]{1,0:T(8,128)(2,1)}) custom-call(bf16[128,2048]{1,0:T(8,128)(2,1)S(1)} %get-tuple-element.308.refs_0_, bf16[128,2048]{1,0:T(8,128)(2,1)S(1)} %get-tuple-element.309.refs_1_, ...), custom_call_target="tpu_custom_call" | custom-call | tf_op jit(solution)/shard_map/cond/branch_0_fun/pallas_call | solution.py:847
Async XLA Ops:
  0.6 90.5 %copy-start.2 = (s32[128]{0:T(128)S(1)}, s32[128]{0:T(128)}, u32[]{:S(2)}) copy-start(s32[128]{0:T(128)} %param.15) | copy-start | bytes 1540
  0.6 90.5 %copy-start.1 = (bf16[128,2048]{1,0:T(8,128)(2,1)S(1)}, bf16[128,2048]{1,0:T(8,128)(2,1)}, u32[]{:S(2)}) copy-start(bf16[128,2048]{1,0:T(8,128)(2,1)} %k_ref.1) | copy-start | bytes 1572868
  0.7 90.5 %copy-start = (bf16[128,2048]{1,0:T(8,128)(2,1)S(1)}, bf16[128,2048]{1,0:T(8,128)(2,1)}, u32[]{:S(2)}) copy-start(bf16[128,2048]{1,0:T(8,128)(2,1)} %q_ref.1) | copy-start | bytes 1572868

commit v4 on v1

--- a/solution.py
+++ b/solution.py
@@ -223,9 +223,9 @@
 
     eight = []
     for by_x, by_z, by_clu in zip(
-        zip((3, 2, 3, 1, 3, 0, 2, 0), (2, 2, 1, 0, 2, 3, 0, 2)),
-        zip((0, 0, 2, 3, 1, 2, 3, 1), (2, 2, 0, 1, 3, 0, 0, 2)),
-        zip((2, 1, 3, 0, 6, 4, 5, 7), (6, 5, 7, 4, 2, 0, 1, 3)),
+        zip((3, 2, 1, 2, 3, 0, 2, 0), (1, 2, 0, 1, 2, 3, 0, 2)),
+        zip((0, 0, 3, 2, 1, 2, 3, 1), (2, 2, 1, 0, 3, 0, 0, 2)),
+        zip((2, 1, 0, 3, 6, 4, 5, 7), (6, 5, 4, 7, 2, 0, 1, 3)),
     ):
         y = lax.rem(at_y + by_core(by_clu[0] // 2, by_clu[1] // 2), 4)
         core = lax.rem(at_core + by_core(by_clu[0] % 2, by_clu[1] % 2), 2)
@@ -238,7 +238,7 @@
             z = at_z + lax.rem(by, 4)
             for j, (more_x, more_z, clu_to) in enumerate(eight):
                 seq_to = lax.rem(x + more_x, 4) * 4 + lax.rem(z + more_z, 4)
-                if j in (3, 5):
+                if j in (2, 5):
                     pl.when(seq_to * groups + clu_to != me)(lambda: visit(seq_to, clu_to))
                 else:
                     visit(seq_to, clu_to)

time: 92.7 us -> 91.4 us (0.986); the launches traced: 91 us -> 91.2 us
  no operation moved by 1% of the time
where the time goes in v4:
time: 91.4 us; the launch traced here: 91.2 us
  Pallas kernels  89.5 us (98%)
  between operations  1.56 us (2%)
    pallas_call x1, Pallas kernels, fast_path(): pl.pallas_call(fast_kernel, out_shape=[rows] * 4 + [jax.ShapeDtypeStruct(...  88.1 us

profile of v4, /device:TPU:1, one launch (start us, length us, event | category | flops | bytes accessed | tf_op | source)
XLA Modules:
  0.0 91.2 jit_solution(16702021775949015196)
XLA Ops:
  0.6 0.0 copy-start.2
  0.6 0.0 copy-start.1
  0.7 0.0 copy-start
  0.7 88.1 %shard_map.92 = (bf16[128,2048]{1,0:T(8,128)(2,1)S(1)}, bf16[128,2048]{1,0:T(8,128)(2,1)S(1)}, bf16[128,2048]{1,0:T(8,128)(2,1)S(1)}, bf16[128,2048]{1,0:T(8,128)(2,1)S(1)}, s32[1,1]{1,0:T(1,128)}) custom-call(s32[1,128]{1,0:T(1,128)} %bitcast.25, bf16[128,2048]{1,0:T(8,128)(2,1)} %q_ref.1, bf16[128,2048]{1,0:T(8,128)(2,1)} %k_ref.1, ...), custom_call_target="tpu_custom_call" | custom-call | tf_op jit(solution)/shard_map/pallas_call | solution.py:777
  89.5 0.0 copy-done.2
  89.5 0.0 copy-done.1
  89.5 0.0 copy-done
  89.5 1.5 %conditional.1 = ((bf16[128,2048]{1,0:T(8,128)(2,1)}, bf16[128,2048]{1,0:T(8,128)(2,1)}, bf16[128,2048]{1,0:T(8,128)(2,1)}, bf16[128,2048]{1,0:T(8,128)(2,1)})) conditional(s32[]{:T(128)} %bitcast.5, (bf16[128,2048]{1,0:T(8,128)(2,1)S(1)}, bf16[128,2048]{1,0:T(8,128)(2,1)S(1)}, bf16[128,2048]{1,0:T(8,128)(2,1)S(1)}, ...), branch_computations={%region_0.0_spmd, %region_1.20_spmd} | conditional | flops 493620608 | bytes 234142496 | solution.py:859
  89.5 1.3 %branch_0_fun.1 = (bf16[128,2048]{1,0:T(8,128)(2,1)}, bf16[128,2048]{1,0:T(8,128)(2,1)}, bf16[128,2048]{1,0:T(8,128)(2,1)}, bf16[128,2048]{1,0:T(8,128)(2,1)}) custom-call(bf16[128,2048]{1,0:T(8,128)(2,1)S(1)} %get-tuple-element.308.refs_0_, bf16[128,2048]{1,0:T(8,128)(2,1)S(1)} %get-tuple-element.309.refs_1_, ...), custom_call_target="tpu_custom_call" | custom-call | tf_op jit(solution)/shard_map/cond/branch_0_fun/pallas_call | solution.py:847
Async XLA Ops:
  0.6 88.8 %copy-start.2 = (s32[128]{0:T(128)S(1)}, s32[128]{0:T(128)}, u32[]{:S(2)}) copy-start(s32[128]{0:T(128)} %param.15) | copy-start | bytes 1540
  0.6 88.8 %copy-start.1 = (bf16[128,2048]{1,0:T(8,128)(2,1)S(1)}, bf16[128,2048]{1,0:T(8,128)(2,1)}, u32[]{:S(2)}) copy-start(bf16[128,2048]{1,0:T(8,128)(2,1)} %k_ref.1) | copy-start | bytes 1572868
  0.7 88.8 %copy-start = (bf16[128,2048]{1,0:T(8,128)(2,1)S(1)}, bf16[128,2048]{1,0:T(8,128)(2,1)}, u32[]{:S(2)}) copy-start(bf16[128,2048]{1,0:T(8,128)(2,1)} %q_ref.1) | copy-start | bytes 1572868

commit v5 on v4

--- a/solution.py
+++ b/solution.py
@@ -223,7 +223,7 @@
 
     eight = []
     for by_x, by_z, by_clu in zip(
-        zip((3, 2, 1, 2, 3, 0, 2, 0), (1, 2, 0, 1, 2, 3, 0, 2)),
+        zip((2, 2, 1, 2, 3, 0, 2, 0), (1, 1, 0, 1, 2, 3, 0, 2)),
         zip((0, 0, 3, 2, 1, 2, 3, 1), (2, 2, 1, 0, 3, 0, 0, 2)),
         zip((2, 1, 0, 3, 6, 4, 5, 7), (6, 5, 4, 7, 2, 0, 1, 3)),
     ):

time: 91.4 us -> 92.6 us (1.013)
  no operation moved by 1% of the time
where the time goes in v5:
time: 92.6 us; the launch traced here: 91.5 us
  Pallas kernels  89.6 us (97%)
  between operations  1.58 us (2%)
    pallas_call x1, Pallas kernels, fast_path(): pl.pallas_call(fast_kernel, out_shape=[rows] * 4 + [jax.ShapeDtypeStruct(...  88.3 us

profile of v5, /device:TPU:1, one launch (start us, length us, event | category | flops | bytes accessed | tf_op | source)
XLA Modules:
  0.0 91.5 jit_solution(10768301327499571861)
XLA Ops:
  0.6 0.0 copy-start.2
  0.6 0.0 copy-start.1
  0.7 0.0 copy-start
  0.7 88.3 %shard_map.92 = (bf16[128,2048]{1,0:T(8,128)(2,1)S(1)}, bf16[128,2048]{1,0:T(8,128)(2,1)S(1)}, bf16[128,2048]{1,0:T(8,128)(2,1)S(1)}, bf16[128,2048]{1,0:T(8,128)(2,1)S(1)}, s32[1,1]{1,0:T(1,128)}) custom-call(s32[1,128]{1,0:T(1,128)} %bitcast.25, bf16[128,2048]{1,0:T(8,128)(2,1)} %q_ref.1, bf16[128,2048]{1,0:T(8,128)(2,1)} %k_ref.1, ...), custom_call_target="tpu_custom_call" | custom-call | tf_op jit(solution)/shard_map/pallas_call | solution.py:777
  89.7 0.0 copy-done.2
  89.7 0.0 copy-done.1
  89.7 0.0 copy-done
  89.7 1.6 %conditional.1 = ((bf16[128,2048]{1,0:T(8,128)(2,1)}, bf16[128,2048]{1,0:T(8,128)(2,1)}, bf16[128,2048]{1,0:T(8,128)(2,1)}, bf16[128,2048]{1,0:T(8,128)(2,1)})) conditional(s32[]{:T(128)} %bitcast.5, (bf16[128,2048]{1,0:T(8,128)(2,1)S(1)}, bf16[128,2048]{1,0:T(8,128)(2,1)S(1)}, bf16[128,2048]{1,0:T(8,128)(2,1)S(1)}, ...), branch_computations={%region_0.0_spmd, %region_1.20_spmd} | conditional | flops 493620608 | bytes 234142496 | solution.py:859
  89.7 1.3 %branch_0_fun.1 = (bf16[128,2048]{1,0:T(8,128)(2,1)}, bf16[128,2048]{1,0:T(8,128)(2,1)}, bf16[128,2048]{1,0:T(8,128)(2,1)}, bf16[128,2048]{1,0:T(8,128)(2,1)}) custom-call(bf16[128,2048]{1,0:T(8,128)(2,1)S(1)} %get-tuple-element.308.refs_0_, bf16[128,2048]{1,0:T(8,128)(2,1)S(1)} %get-tuple-element.309.refs_1_, ...), custom_call_target="tpu_custom_call" | custom-call | tf_op jit(solution)/shard_map/cond/branch_0_fun/pallas_call | solution.py:847
Async XLA Ops:
  0.6 89.0 %copy-start.2 = (s32[128]{0:T(128)S(1)}, s32[128]{0:T(128)}, u32[]{:S(2)}) copy-start(s32[128]{0:T(128)} %param.15) | copy-start | bytes 1540
  0.6 89.0 %copy-start.1 = (bf16[128,2048]{1,0:T(8,128)(2,1)S(1)}, bf16[128,2048]{1,0:T(8,128)(2,1)}, u32[]{:S(2)}) copy-start(bf16[128,2048]{1,0:T(8,128)(2,1)} %k_ref.1) | copy-start | bytes 1572868
  0.7 89.0 %copy-start = (bf16[128,2048]{1,0:T(8,128)(2,1)S(1)}, bf16[128,2048]{1,0:T(8,128)(2,1)}, u32[]{:S(2)}) copy-start(bf16[128,2048]{1,0:T(8,128)(2,1)} %q_ref.1) | copy-start | bytes 1572868

commit v6 on v3

--- a/solution.py
+++ b/solution.py
@@ -223,9 +223,9 @@
 
     eight = []
     for by_x, by_z, by_clu in zip(
-        zip((3, 2, 3, 1, 3, 0, 2, 0), (2, 2, 1, 0, 2, 3, 0, 2)),
-        zip((0, 0, 2, 3, 1, 2, 3, 1), (2, 2, 0, 1, 3, 0, 0, 2)),
-        zip((2, 1, 3, 0, 6, 4, 5, 7), (6, 5, 7, 4, 2, 0, 1, 3)),
+        zip((3, 2, 1, 2, 3, 0, 2, 0), (1, 2, 0, 1, 2, 3, 0, 2)),
+        zip((0, 0, 3, 2, 1, 2, 3, 1), (2, 2, 1, 0, 3, 0, 0, 2)),
+        zip((2, 1, 0, 3, 6, 4, 5, 7), (6, 5, 4, 7, 2, 0, 1, 3)),
     ):
         y = lax.rem(at_y + by_core(by_clu[0] // 2, by_clu[1] // 2), 4)
         core = lax.rem(at_core + by_core(by_clu[0] % 2, by_clu[1] % 2), 2)
@@ -238,7 +238,7 @@
             z = at_z + lax.rem(by, 4)
             for j, (more_x, more_z, clu_to) in enumerate(eight):
                 seq_to = lax.rem(x + more_x, 4) * 4 + lax.rem(z + more_z, 4)
-                if j in (3, 5):
+                if j in (2, 5):
                     pl.when(seq_to * groups + clu_to != me)(lambda: visit(seq_to, clu_to))
                 else:
                     visit(seq_to, clu_to)
@@ -413,7 +413,6 @@
 
         return carry
 
-    lax.fori_loop(0, heads, send_heavy, 0)
     along_seq(lambda to: ex_send.at[to], ex_recv, ex_send_sem, ex_recv_sem)
     out_a = (send_a, recv_a.at[me], send_a_sem, recv_a_sem)
     send_steps(0, 4, *out_a)
@@ -421,6 +420,7 @@
     along_seq(lambda to: cnt_group, cnt_recv, cnt2_send_sem, cnt2_sem)
     send_steps(4, devices // 8 - 4, *out_a)
     send_own(send_a, recv_a.at[me], recv_a_sem)
+    lax.fori_loop(0, heads, send_heavy, 0)
 
     for tile in range(1, 4):
         put_pack((tile + 1) * TOK + 48, TOK, tile_picks(tile))

time: 93.5 us -> 100 us (1.070)
  Pallas kernels: 91.2 us -> 96.9 us
    pallas_call x1, Pallas kernels: 89.8 us -> 95.6 us  [fast_path(): pl.pallas_call(fast_kernel, out_shape=[rows] * 4 + [jax.ShapeDtypeStruct(...]
where the time goes in v6:
time: 100 us; the launch traced here: 98.8 us
  Pallas kernels  96.9 us (97%)
  between operations  1.58 us (2%)
    pallas_call x1, Pallas kernels, fast_path(): pl.pallas_call(fast_kernel, out_shape=[rows] * 4 + [jax.ShapeDtypeStruct(...  95.6 us

profile of v6, /device:TPU:1, one launch (start us, length us, event | category | flops | bytes accessed | tf_op | source)
XLA Modules:
  0.0 98.8 jit_solution(5638615905496017188)
XLA Ops:
  0.6 0.0 copy-start.2
  0.6 0.0 copy-start.1
  0.7 0.0 copy-start
  0.7 95.6 %shard_map.92 = (bf16[128,2048]{1,0:T(8,128)(2,1)S(1)}, bf16[128,2048]{1,0:T(8,128)(2,1)S(1)}, bf16[128,2048]{1,0:T(8,128)(2,1)S(1)}, bf16[128,2048]{1,0:T(8,128)(2,1)S(1)}, s32[1,1]{1,0:T(1,128)}) custom-call(s32[1,128]{1,0:T(1,128)} %bitcast.25, bf16[128,2048]{1,0:T(8,128)(2,1)} %q_ref.1, bf16[128,2048]{1,0:T(8,128)(2,1)} %k_ref.1, ...), custom_call_target="tpu_custom_call" | custom-call | tf_op jit(solution)/shard_map/pallas_call | solution.py:777
  96.9 0.0 copy-done.2
  96.9 0.0 copy-done.1
  96.9 0.0 copy-done
  97.0 1.6 %conditional.1 = ((bf16[128,2048]{1,0:T(8,128)(2,1)}, bf16[128,2048]{1,0:T(8,128)(2,1)}, bf16[128,2048]{1,0:T(8,128)(2,1)}, bf16[128,2048]{1,0:T(8,128)(2,1)})) conditional(s32[]{:T(128)} %bitcast.5, (bf16[128,2048]{1,0:T(8,128)(2,1)S(1)}, bf16[128,2048]{1,0:T(8,128)(2,1)S(1)}, bf16[128,2048]{1,0:T(8,128)(2,1)S(1)}, ...), branch_computations={%region_0.0_spmd, %region_1.20_spmd} | conditional | flops 493620608 | bytes 234142496 | solution.py:859
  97.0 1.3 %branch_0_fun.1 = (bf16[128,2048]{1,0:T(8,128)(2,1)}, bf16[128,2048]{1,0:T(8,128)(2,1)}, bf16[128,2048]{1,0:T(8,128)(2,1)}, bf16[128,2048]{1,0:T(8,128)(2,1)}) custom-call(bf16[128,2048]{1,0:T(8,128)(2,1)S(1)} %get-tuple-element.308.refs_0_, bf16[128,2048]{1,0:T(8,128)(2,1)S(1)} %get-tuple-element.309.refs_1_, ...), custom_call_target="tpu_custom_call" | custom-call | tf_op jit(solution)/shard_map/cond/branch_0_fun/pallas_call | solution.py:847
Async XLA Ops:
  0.6 96.3 %copy-start.2 = (s32[128]{0:T(128)S(1)}, s32[128]{0:T(128)}, u32[]{:S(2)}) copy-start(s32[128]{0:T(128)} %param.15) | copy-start | bytes 1540
  0.6 96.3 %copy-start.1 = (bf16[128,2048]{1,0:T(8,128)(2,1)S(1)}, bf16[128,2048]{1,0:T(8,128)(2,1)}, u32[]{:S(2)}) copy-start(bf16[128,2048]{1,0:T(8,128)(2,1)} %k_ref.1) | copy-start | bytes 1572868
  0.7 96.3 %copy-start = (bf16[128,2048]{1,0:T(8,128)(2,1)S(1)}, bf16[128,2048]{1,0:T(8,128)(2,1)}, u32[]{:S(2)}) copy-start(bf16[128,2048]{1,0:T(8,128)(2,1)} %q_ref.1) | copy-start | bytes 1572868
